TPU v7x, 512 devices: a whole 4x4x16 slice. The times are simulated.
512 devices in a mesh: leaf: 32 (over y, x, core), front: 16 (over z).
Axes of the slice: x: 4, y: 4, z: 16, core: 2. Of those that a mesh axis runs over, the one named last changes fastest.
Arguments:
- leaf_pivot_block: bfloat16 [32, 2048, 256], P('leaf', 'front'), may hold values from -6 to 6
- leaf_rest_block: bfloat16 [32, 512, 256], P('leaf', 'front'), may hold values from -6 to 6
- node_pivot_block: bfloat16 [32, 2048, 256], P('leaf', 'front'), may hold values from -6 to 6
- node_rest_block: bfloat16 [32, 512, 256], P('leaf', 'front'), may hold values from -6 to 6
- leaf_vectors_pivot: bfloat16 [32, 2, 2048, 2048], P('leaf', None, 'front'), may hold values from -0.125 to 0.125
- leaf_vectors_rest: bfloat16 [32, 2, 512, 2048], P('leaf', None, 'front'), may hold values from -0.125 to 0.125
- node_vectors_pivot: bfloat16 [32, 2, 2048, 2048], P('leaf', None, 'front'), may hold values from -0.125 to 0.125
- node_vectors_rest: bfloat16 [32, 2, 512, 2048], P('leaf', None, 'front'), may hold values from -0.125 to 0.125
- stack_place: int32 [32, 1024], P('leaf'), may hold values from 0 to 2559, as said below
- parent_columns: int32 [32, 2, 512], P('leaf'), may hold values from 0 to 2047, as said below
- coupling: bfloat16 [32, 2, 2048, 512], P('leaf', None, 'front'), may hold values from -0.125 to 0.125
- pivot_inverse: bfloat16 [32, 2, 2048, 2048], P('leaf', None, 'front'), may hold values from -0.125 to 0.125
Outputs:
- solution: bfloat16 [32, 2, 2048, 256], P('leaf', None, 'front')
- remainder: bfloat16 [32, 512, 256], P('leaf', 'front')
Inputs may be any that keep to these rules, and one draw needn't show every extreme that they name: `stack_place`: each group's row holds 1024 distinct stack rows. `parent_columns`: each group's row for each slot holds 512 distinct pivot columns.
All inputs are finite; a program needn't handle non-finite values.
Results may differ from a plain program's by a relative error of at most 0.024.
Values may be sent and summed in bfloat16 or wider, within the bound.
No kernel may reach another device: no remote copies, remote signals or barrier semaphores. Data moves between devices by JAX's collectives and lax.ppermute only.
A program may use at most 64 MiB of HBM per device.

v0:
```python
import jax
import jax.numpy as jnp
from jax import lax
from jax.sharding import PartitionSpec as P

K = 2048
C = 512
LEVELS = 2


def in_one_piece(arrays, axis, dim, along):
    ends, at = ([], 0)
    for a in arrays[:-1]:
        at += a.shape[along]
        ends.append(at)
    both = jnp.concatenate(arrays, axis=along)
    return tuple(jnp.split(lax.all_gather(both, axis, axis=dim, tiled=True), ends, axis=along))


def from_behind(block, axis, distance):
    devices = range(lax.axis_size(axis))
    route = [((i - distance) % len(devices), i) for i in devices]
    return lax.ppermute(block, axis, route)


def laid_out(parts, dim):
    lengths = list(parts.shape[1:])
    lengths[dim] *= parts.shape[0]
    return jnp.moveaxis(parts, 0, dim).reshape(lengths)


def sent_to_all(shard, axis):
    copies = jnp.broadcast_to(shard, (lax.axis_size(axis), *shard.shape))
    return lax.all_to_all(copies, axis, split_axis=0, concat_axis=0, tiled=True)


def gather_directly(shard, axis, dim):
    return laid_out(sent_to_all(shard, axis), dim)


def added(first, second):
    return (first.astype(jnp.float32) + second.astype(jnp.float32)).astype(jnp.bfloat16)


def per_device(
    leaf_pivot_block,
    leaf_rest_block,
    node_pivot_block,
    node_rest_block,
    leaf_vectors_pivot,
    leaf_vectors_rest,
    node_vectors_pivot,
    node_vectors_rest,
    stack_place,
    parent_columns,
    coupling,
    pivot_inverse,
):
    subtree = 2**LEVELS
    front_index = lax.axis_index("front")
    pivot_count = leaf_vectors_pivot.shape[2]
    rest_count = leaf_vectors_rest.shape[2]

    def reflect(block_pivot, block_rest, vectors_pivot, vectors_rest):
        partial_value = jnp.einsum(
            "ik,ir->kr", vectors_pivot[1], block_pivot, preferred_element_type=jnp.float32
        )
        partial_value = partial_value + jnp.einsum(
            "ik,ir->kr", vectors_rest[1], block_rest, preferred_element_type=jnp.float32
        )
        summed = lax.psum(partial_value.astype(jnp.bfloat16), "front")
        pivots = block_pivot - jnp.dot(vectors_pivot[0], summed, preferred_element_type=jnp.float32)
        rest = block_rest - jnp.dot(vectors_rest[0], summed, preferred_element_type=jnp.float32)
        return (pivots.astype(jnp.bfloat16), rest.astype(jnp.bfloat16))

    inverse_map = (
        jnp.full((K + C,), -1, jnp.int32).at[stack_place[0]].set(jnp.arange(2 * C, dtype=jnp.int32))
    )
    pivot_rows = front_index * pivot_count + jnp.arange(pivot_count, dtype=jnp.int32)
    rest_rows = K + front_index * rest_count + jnp.arange(rest_count, dtype=jnp.int32)
    pivot_source = inverse_map[pivot_rows]
    rest_source = inverse_map[rest_rows]

    def assemble(left_part, right_part):
        left_whole, right_whole = in_one_piece((left_part, right_part), "front", 0, 1)
        joined = jnp.concatenate([left_whole, right_whole], axis=0)

        def fill_rows(own_rows, source):
            picked_rows = jnp.take(joined, jnp.maximum(source, 0), axis=0)
            return jnp.where((source >= 0)[:, None], picked_rows, own_rows)

        return (
            fill_rows(node_pivot_block[0], pivot_source),
            fill_rows(node_rest_block[0], rest_source),
        )

    def run_node(left_part, right_part):
        stack_pivots, stack_rest = assemble(left_part, right_part)
        return reflect(stack_pivots, stack_rest, node_vectors_pivot[0], node_vectors_rest[0])

    leaf_pivots, leaf_remainder = reflect(
        leaf_pivot_block[0], leaf_rest_block[0], leaf_vectors_pivot[0], leaf_vectors_rest[0]
    )
    left_part = from_behind(leaf_remainder, "leaf", 1)
    node_pivots, node_remainder = run_node(left_part, leaf_remainder)
    height = 2
    offset = 2 ** (height - 2)
    left_part = from_behind(node_remainder, "leaf", offset)
    right_part = from_behind(node_remainder, "leaf", -offset)
    node_pivots, node_remainder = run_node(left_part, right_part)
    root_part = from_behind(node_remainder, "leaf", -(subtree // 2))
    node_pivots, node_remainder = run_node(root_part, jnp.zeros_like(root_part))
    pivots_all, coupling_all = in_one_piece(
        (jnp.stack([leaf_pivots, node_pivots]), coupling[0]), "front", 1, 2
    )

    def settle(which_slot, parent, columns):
        right_side = pivots_all[which_slot].astype(jnp.float32)
        if parent is not None:
            chosen = jnp.take(parent, columns, axis=0)
            right_side = right_side - jnp.dot(
                coupling_all[which_slot], chosen, preferred_element_type=jnp.float32
            )
        result = jnp.dot(
            pivot_inverse[0, which_slot],
            right_side.astype(jnp.bfloat16),
            preferred_element_type=jnp.float32,
        )
        return result.astype(jnp.bfloat16)

    def fetch_parent(parent_part):
        return gather_directly(parent_part, "front", 0)

    node_solution = settle(1, None, None)
    for height in range(LEVELS, 0, -1):
        if height == LEVELS:
            parent_part = from_behind(node_solution, "leaf", subtree // 2)
        else:
            offset = 2 ** (height - 1)
            lower_part = from_behind(node_solution, "leaf", offset)
            higher_part = from_behind(node_solution, "leaf", -offset)
            parent_part = added(higher_part, lower_part)
        node_solution = settle(1, fetch_parent(parent_part), parent_columns[0, 1])
    from_right = from_behind(node_solution, "leaf", -1)
    parent_part = added(from_right, node_solution)
    leaf_solution = settle(0, fetch_parent(parent_part), parent_columns[0, 0])
    solution = jnp.stack([leaf_solution, node_solution])[None]
    return (solution, node_remainder[None])


def solution(mesh):
    in_specs = (
        P("leaf", "front", None),
        P("leaf", "front", None),
        P("leaf", "front", None),
        P("leaf", "front", None),
        P("leaf", None, "front", None),
        P("leaf", None, "front", None),
        P("leaf", None, "front", None),
        P("leaf", None, "front", None),
        P("leaf", None),
        P("leaf", None, None),
        P("leaf", None, "front", None),
        P("leaf", None, "front", None),
    )
    out_specs = (P("leaf", None, "front", None), P("leaf", "front", None))
    return jax.shard_map(
        per_device, mesh=mesh, in_specs=in_specs, out_specs=out_specs, check_vma=False
    )
```

profile of v0, /device:TPU:127, one launch (start us, length us, event | category | flops | bytes accessed | tf_op | source)
XLA Modules:
  0.0 993.0 jit_solution(9829018714895478358)
XLA Ops:
  10.4 4.3 scatter_custom_fusion
  16.7 125.2 %all-reduce.6.cloned.1.call-done = bf16[2048,256]{1,0:T(8,128)(2,1)} async-done(((bf16[2048,256]{1,0:T(8,128)(2,1)}), bf16[2048,256]{1,0:T(8,128)(2,1)}) %all-reduce.6.cloned.1.call-update) | async-done | bytes 1048592 | tf_op jit(solution)/shard_map/psum | solution.py:71
  143.4 12.0 %collective-permute-start = (bf16[32,256]{1,0:T(8,128)(2,1)S(1)}, bf16[32,256]{1,0:T(8,128)(2,1)S(1)}, u32[]{:S(2)}, u32[]{:S(2)}) collective-permute-start(bf16[32,256]{1,0:T(8,128)(2,1)S(1)} %fusion.32), channel_id=1, source_target_pairs={{496,0},{0,16},{16,32},{32,48},{48,64},{64,80},{80,96},{96,112},{1... | collective-permute-start | bytes 49160 | tf_op jit(solution)/shard_map/ppermute | solution.py:23
  156.3 22.6 %all_gather.12 = bf16[512,512]{1,0:T(8,128)(2,1)S(1)} all-gather(bf16[32,512]{1,0:T(8,128)(2,1)S(1)} %pad_maximum_fusion.5), channel_id=1, replica_groups=mesh['leaf'=32,'front'=16] {'front'}, dimensions={0}, use_global_device_ids=true | all-gather | bytes 557056 | tf_op jit(solution)/shard_map/all_gather | solution.py:17
  182.7 135.9 %all-reduce.8.cloned.1.call-done = bf16[2048,256]{0,1:T(8,128)(2,1)} async-done(((bf16[2048,256]{0,1:T(8,128)(2,1)}), bf16[2048,256]{0,1:T(8,128)(2,1)}) %all-reduce.8.cloned.1.call-update) | async-done | bytes 1048592 | tf_op jit(solution)/shard_map/psum | solution.py:71
  320.2 11.9 %collective-permute-start.1 = (bf16[32,256]{1,0:T(8,128)(2,1)S(1)}, bf16[32,256]{1,0:T(8,128)(2,1)S(1)}, u32[]{:S(2)}, u32[]{:S(2)}) collective-permute-start(bf16[32,256]{1,0:T(8,128)(2,1)S(1)} %fusion.29), channel_id=1, source_target_pairs={{496,0},{0,16},{16,32},{32,48},{48,64},{64,80},{80,96},{96,112},{1... | collective-permute-start | bytes 49160 | tf_op jit(solution)/shard_map/ppermute | solution.py:23
  332.1 1.9 collective-permute-start.2
  334.1 6.4 collective-permute-done.2
  340.5 22.1 %all_gather.13 = bf16[512,512]{1,0:T(8,128)(2,1)S(1)} all-gather(bf16[32,512]{1,0:T(8,128)(2,1)S(1)} %pad_maximum_fusion.6), channel_id=1, replica_groups=mesh['leaf'=32,'front'=16] {'front'}, dimensions={0}, use_global_device_ids=true | all-gather | bytes 557056 | tf_op jit(solution)/shard_map/all_gather | solution.py:17
  366.3 130.4 %all-reduce.10.cloned.1.call-done = bf16[2048,256]{0,1:T(8,128)(2,1)} async-done(((bf16[2048,256]{0,1:T(8,128)(2,1)}), bf16[2048,256]{0,1:T(8,128)(2,1)}) %all-reduce.10.cloned.1.call-update) | async-done | bytes 1048592 | tf_op jit(solution)/shard_map/psum | solution.py:71
  498.3 2.5 collective-permute-start.3
  500.8 5.3 collective-permute-done.3
  506.1 22.5 %all_gather.14 = bf16[512,512]{1,0:T(8,128)(2,1)S(1)} all-gather(bf16[32,512]{1,0:T(8,128)(2,1)S(1)} %concatenate.25), channel_id=1, replica_groups=mesh['leaf'=32,'front'=16] {'front'}, dimensions={0}, use_global_device_ids=true | all-gather | bytes 557056 | tf_op jit(solution)/shard_map/all_gather | solution.py:17
  534.1 142.4 %all-reduce.12.cloned.1.call-done = bf16[2048,256]{0,1:T(8,128)(2,1)} async-done(((bf16[2048,256]{0,1:T(8,128)(2,1)}), bf16[2048,256]{0,1:T(8,128)(2,1)}) %all-reduce.12.cloned.1.call-update) | async-done | bytes 1048592 | tf_op jit(solution)/shard_map/psum | solution.py:71
  679.1 89.4 %all-gather.2.cloned.1.call-done = bf16[2,2048,768]{2,1,0:T(8,128)(2,1)} async-done(((bf16[2,128,768]{2,1,0:T(8,128)(2,1)}), bf16[2,2048,768]{2,1,0:T(8,128)(2,1)}) %all-gather.2.cloned.1.call-update) | async-done | bytes 6291472 | tf_op jit(solution)/shard_map/all_gather | solution.py:17
  770.2 2.1 collective-permute-start.4
  772.3 2.9 collective-permute-done.4
  776.5 11.0 %all-to-all-start = ((bf16[16,128,256]{2,1,0:T(8,128)(2,1)}), bf16[16,128,256]{2,1,0:T(8,128)(2,1)S(1)}, u32[]{:S(2)}, u32[]{:S(2)}) async-start(bf16[16,128,256]{2,1,0:T(8,128)(2,1)} %broadcast_in_dim.86), calls=%async_computation | async-start | bytes 2097152 | tf_op jit(solution)/shard_map/all_to_all | solution.py:34
  787.6 46.8 %all-to-all-done = bf16[16,128,256]{2,1,0:T(8,128)(2,1)S(1)} async-done(((bf16[16,128,256]{2,1,0:T(8,128)(2,1)}), bf16[16,128,256]{2,1,0:T(8,128)(2,1)S(1)}, u32[]{:S(2)}, u32[]{:S(2)}) %all-to-all-start) | async-done | bytes 1048608 | tf_op jit(solution)/shard_map/all_to_all | solution.py:34
  834.4 1.9 gather_fusion.8
  836.3 3.3 fusion.21
  839.6 4.3 collective-permute-start.5
  844.0 5.3 collective-permute-start.6
  850.8 60.4 %all_to_all.15 = bf16[16,128,256]{2,1,0:T(8,128)(2,1)S(1)} all-to-all(bf16[16,128,256]{2,1,0:T(8,128)(2,1)S(1)} %broadcast_in_dim.87), channel_id=1, replica_groups=mesh['leaf'=32,'front'=16] {'front'}, dimensions={0} | all-to-all | bytes 2097152 | tf_op jit(solution)/shard_map/all_to_all | solution.py:34
  911.2 1.9 gather_fusion.9
  913.2 3.3 fusion.19
  916.5 2.1 collective-permute-start.7
  918.5 7.0 collective-permute-done.7
  926.8 6.7 all-to-all-start.2
  934.6 45.9 %all-to-all-done.2 = bf16[16,128,256]{2,1,0:T(8,128)(2,1)S(1)} async-done(((bf16[16,128,256]{2,1,0:T(8,128)(2,1)}), bf16[16,128,256]{2,1,0:T(8,128)(2,1)S(1)}, u32[]{:S(2)}, u32[]{:S(2)}) %all-to-all-start.2) | async-done | bytes 1048608 | tf_op jit(solution)/shard_map/all_to_all | solution.py:34
  980.5 1.9 gather_fusion.10
  982.4 3.3 fusion.22
  (109 shorter events, 33.6 us)
Async XLA Ops:
  7.2 1.6 copy-start.8
  7.2 1.6 copy-start.5
  7.2 134.7 %all-reduce.6.cloned.1.call-start = ((), (), s32[]{:S(2)}) async-start(), calls=%async_computation.3 | async-start | bytes 2097152 | tf_op jit(solution)/shard_map/psum | solution.py:71
  8.8 1.6 copy-start.10
  10.3 145.2 %copy-start.9 = (bf16[1,128,256]{2,1,0:T(8,128)(2,1)S(1)}, bf16[1,128,256]{2,1,0:T(8,128)(2,1)}, u32[]{:S(2)}) copy-start(bf16[1,128,256]{2,1,0:T(8,128)(2,1)} %param.20) | copy-start | bytes 196612
  10.3 308.3 %all-reduce.8.cloned.1.call-start = ((), (), s32[]{:S(2)}) async-start(), calls=%async_computation.4 | async-start | bytes 2097152 | tf_op jit(solution)/shard_map/psum | solution.py:71
  143.4 37.2 %copy-start = (bf16[1,2,128,2048]{3,2,1,0:T(8,128)(2,1)S(1)}, bf16[1,2,128,2048]{3,2,1,0:T(8,128)(2,1)}, u32[]{:S(2)}) copy-start(bf16[1,2,128,2048]{3,2,1,0:T(8,128)(2,1)} %param.24) | copy-start | bytes 3145732
  143.4 12.9 %collective-permute-start = (bf16[32,256]{1,0:T(8,128)(2,1)S(1)}, bf16[32,256]{1,0:T(8,128)(2,1)S(1)}, u32[]{:S(2)}, u32[]{:S(2)}) collective-permute-start(bf16[32,256]{1,0:T(8,128)(2,1)S(1)} %fusion.32), channel_id=1, source_target_pairs={{496,0},{0,16},{16,32},{32,48},{48,64},{64,80},{80,96},{96,112},{1... | collective-permute-start | bytes 49160 | tf_op jit(solution)/shard_map/ppermute | solution.py:23
  179.0 2.1 copy-start.1
  179.0 2.1 copy-start.4
  182.6 314.0 %all-reduce.10.cloned.1.call-start = ((), (), s32[]{:S(2)}) async-start(), calls=%async_computation.5 | async-start | bytes 2097152 | tf_op jit(solution)/shard_map/psum | solution.py:71
  320.2 13.8 %collective-permute-start.1 = (bf16[32,256]{1,0:T(8,128)(2,1)S(1)}, bf16[32,256]{1,0:T(8,128)(2,1)S(1)}, u32[]{:S(2)}, u32[]{:S(2)}) collective-permute-start(bf16[32,256]{1,0:T(8,128)(2,1)S(1)} %fusion.29), channel_id=1, source_target_pairs={{496,0},{0,16},{16,32},{32,48},{48,64},{64,80},{80,96},{96,112},{1... | collective-permute-start | bytes 49160 | tf_op jit(solution)/shard_map/ppermute | solution.py:23
  332.1 8.4 collective-permute-start.2
  366.3 310.2 %all-reduce.12.cloned.1.call-start = ((), (), s32[]{:S(2)}) async-start(), calls=%async_computation.6 | async-start | bytes 2097152 | tf_op jit(solution)/shard_map/psum | solution.py:71
  498.3 7.8 collective-permute-start.3
  530.7 1.6 copy-start.7
  530.8 1.7 copy-start.2
  532.3 236.2 %all-gather.2.cloned.1.call-start = ((), (), s32[]{:S(2)}) async-start(), calls=%async_computation.7 | async-start | bytes 6684672 | tf_op jit(solution)/shard_map/all_gather | solution.py:17
  532.5 145.8 %copy-start.6 = (bf16[1,2,128,512]{3,2,1,0:T(8,128)(2,1)S(1)}, bf16[1,2,128,512]{3,2,1,0:T(8,128)(2,1)}, u32[]{:S(2)}) copy-start(bf16[1,2,128,512]{3,2,1,0:T(8,128)(2,1)} %param.28) | copy-start | bytes 786436
  534.1 234.4 %copy-start.12 = (bf16[1,2,128,2048]{3,2,1,0:T(8,128)(2,1)S(1)}, bf16[1,2,128,2048]{3,2,1,0:T(8,128)(2,1)}, u32[]{:S(2)}) copy-start(bf16[1,2,128,2048]{3,2,1,0:T(8,128)(2,1)} %param.29) | copy-start | bytes 3145732
  770.2 17.3 %copy-start.11 = (s32[1,2,512]{2,1,0:T(2,128)S(1)}, s32[1,2,512]{2,1,0:T(2,128)}, u32[]{:S(2)}) copy-start(s32[1,2,512]{2,1,0:T(2,128)} %param.27) | copy-start | bytes 12292
  770.2 5.0 collective-permute-start.4
  776.5 57.9 %all-to-all-start = ((bf16[16,128,256]{2,1,0:T(8,128)(2,1)}), bf16[16,128,256]{2,1,0:T(8,128)(2,1)S(1)}, u32[]{:S(2)}, u32[]{:S(2)}) async-start(bf16[16,128,256]{2,1,0:T(8,128)(2,1)} %broadcast_in_dim.86), calls=%async_computation | async-start | bytes 2097152 | tf_op jit(solution)/shard_map/all_to_all | solution.py:34
  839.6 9.7 collective-permute-start.5
  844.0 6.6 collective-permute-start.6
  916.4 17.1 %copy-start.3 = (bf16[2048,256]{0,1:T(8,128)(2,1)S(1)}, bf16[2048,256]{0,1:T(8,128)(2,1)}, u32[]{:S(2)}) copy-start(bf16[2048,256]{0,1:T(8,128)(2,1)} %all-reduce.12.cloned.1.call-done) | copy-start | bytes 3145732
  916.5 9.0 collective-permute-start.7
  926.8 53.7 %all-to-all-start.2 = ((bf16[16,128,256]{2,1,0:T(8,128)(2,1)}), bf16[16,128,256]{2,1,0:T(8,128)(2,1)S(1)}, u32[]{:S(2)}, u32[]{:S(2)}) async-start(bf16[16,128,256]{2,1,0:T(8,128)(2,1)} %broadcast_in_dim.88), calls=%async_computation.2 | async-start | bytes 2097152 | tf_op jit(solution)/shard_map/all_to_all | solution.py:34
Sparse Core Ops, SparseCore 0:
  10.4 131.4 all-reduce.5
  182.8 135.7 all-reduce.7
  366.4 130.2 all-reduce.9
  532.4 143.9 all-reduce.11
  679.2 89.2 all-gather.1
where the time goes:
time: 994 us; the launch traced here: 993 us
  waiting for transfers between devices  740 us (74%)
  blocking collectives  128 us (13%)
  starting transfers between devices  60 us (6%)
  matrix products  29.4 us (3%)
  local copies, waits for them, and re-layouts  20.8 us (2%)
  between operations  14.4 us (1%)
    psum x4, waiting for transfers between devices, reflect(): summed = lax.psum(partial_value.astype(jnp.bfloat16), 'front')  534 us
    all_to_all x2, waiting for transfers between devices, sent_to_all(): return lax.all_to_all(copies, axis, split_axis=0, concat_axis=0, tiled=True)  92.7 us
    all_gather x1, waiting for transfers between devices, in_one_piece(): lax.all_gather(both, axis, axis=dim, tiled=True)  89.4 us
    all_gather x3, blocking collectives, in_one_piece(): lax.all_gather(both, axis, axis=dim, tiled=True)  67.2 us
    all_to_all x1, blocking collectives, sent_to_all(): return lax.all_to_all(copies, axis, split_axis=0, concat_axis=0, tiled=True)  60.4 us
    ppermute x8, starting transfers between devices, from_behind(): return lax.ppermute(block, axis, route)  42.1 us
    ppermute x8, waiting for transfers between devices, from_behind(): return lax.ppermute(block, axis, route)  23.6 us
  transfers between devices with their start and end apart: 15, of which 13 were waited for; matrix products, arithmetic and copies ran while one was open for 1% of the time, Pallas kernels for 0%

commit v1 on v0

--- a/solution.py
+++ b/solution.py
@@ -6,6 +6,11 @@
 K = 2048
 C = 512
 LEVELS = 2
+
+
+def add_all(block, mesh_axis):
+    blocks = lax.all_gather(block, mesh_axis)
+    return jnp.sum(blocks, axis=0)
 
 
 def in_one_piece(arrays, axis, dim, along):
@@ -68,7 +73,7 @@
         partial_value = partial_value + jnp.einsum(
             "ik,ir->kr", vectors_rest[1], block_rest, preferred_element_type=jnp.float32
         )
-        summed = lax.psum(partial_value.astype(jnp.bfloat16), "front")
+        summed = add_all(partial_value.astype(jnp.bfloat16), "front")
         pivots = block_pivot - jnp.dot(vectors_pivot[0], summed, preferred_element_type=jnp.float32)
         rest = block_rest - jnp.dot(vectors_rest[0], summed, preferred_element_type=jnp.float32)
         return (pivots.astype(jnp.bfloat16), rest.astype(jnp.bfloat16))

time: 994 us -> 1290 us (1.30)
  the two profiles are of different devices: /device:TPU:127 before, /device:TPU:13 now
where the time goes in v1:
time: 1290 us
  waiting for transfers between devices  969 us (75%)
  blocking collectives  131 us (10%)
  local copies, waits for them, and re-layouts  68.6 us (5%)
  starting transfers between devices  43 us (3%)
  other arithmetic  34.4 us (3%)
  matrix products  25.7 us (2%)
  between operations  14.6 us (1%)
    all_gather x4, waiting for transfers between devices, add_all(): blocks = lax.all_gather(block, mesh_axis)  779 us
    all_to_all x2, waiting for transfers between devices, sent_to_all(): return lax.all_to_all(copies, axis, split_axis=0, concat_axis=0, tiled=True)  93.9 us
    all_gather x1, waiting for transfers between devices, in_one_piece(): lax.all_gather(both, axis, axis=dim, tiled=True)  82.3 us
    all_gather x3, blocking collectives, in_one_piece(): lax.all_gather(both, axis, axis=dim, tiled=True)  72.2 us
    all_to_all x1, blocking collectives, sent_to_all(): return lax.all_to_all(copies, axis, split_axis=0, concat_axis=0, tiled=True)  59.2 us
    unnamed x48, local copies, waits for them, and re-layouts  48.4 us
    reduce_sum x4, other arithmetic, add_all(): return jnp.sum(blocks, axis=0)  33.3 us
    ppermute x8, starting transfers between devices, from_behind(): return lax.ppermute(block, axis, route)  26.5 us
  transfers between devices with their start and end apart: 15, of which 13 were waited for; matrix products, arithmetic and copies ran while one was open for 1% of the time, Pallas kernels for 0%

profile of v1, /device:TPU:13, one launch (start us, length us, event | category | flops | bytes accessed | tf_op | source)
XLA Modules:
  0.0 1286.5 jit_solution(15286955092665730789)
XLA Ops:
  10.4 4.3 scatter_custom_fusion
  16.7 188.3 %all-gather.12.cloned.1.call-done = bf16[32768,256]{1,0:T(8,128)(2,1)} async-done(((bf16[2048,256]{1,0:T(8,128)(2,1)}), bf16[32768,256]{1,0:T(8,128)(2,1)}) %all-gather.12.cloned.1.call-update) | async-done | bytes 16777232 | tf_op jit(solution)/shard_map/all_gather | solution.py:12
  205.0 8.9 reduce_sum.48
  214.2 3.5 collective-permute-start
  218.5 23.9 %all_gather.38 = bf16[512,512]{1,0:T(8,128)(2,1)S(1)} all-gather(bf16[32,512]{1,0:T(8,128)(2,1)S(1)} %pad_maximum_fusion.5), channel_id=1, replica_groups=mesh['leaf'=32,'front'=16] {'front'}, dimensions={0}, use_global_device_ids=true | all-gather | bytes 557056 | tf_op jit(solution)/shard_map/all_gather | solution.py:22
  246.1 196.5 %all-gather.14.cloned.1.call-done = bf16[32768,256]{0,1:T(8,128)(2,1)} async-done(((bf16[2048,256]{0,1:T(8,128)(2,1)}), bf16[32768,256]{0,1:T(8,128)(2,1)}) %all-gather.14.cloned.1.call-update) | async-done | bytes 16777232 | tf_op jit(solution)/shard_map/all_gather | solution.py:12
  442.7 15.1 %copy.44 = bf16[32,8,16,2048]{3,2,1,0:T(8,128)(2,1)S(1)} copy(bf16[32,8,16,2048]{3,1,2,0:T(8,128)(2,1)} %bitcast.221) | data formatting | bytes 33554432
  457.8 8.1 bitcast_reduce_fusion.2
  466.3 2.6 collective-permute-start.2
  468.9 3.0 collective-permute-start.1
  472.8 24.2 %all_gather.41 = bf16[512,512]{1,0:T(8,128)(2,1)S(1)} all-gather(bf16[32,512]{1,0:T(8,128)(2,1)S(1)} %pad_maximum_fusion.6), channel_id=1, replica_groups=mesh['leaf'=32,'front'=16] {'front'}, dimensions={0}, use_global_device_ids=true | all-gather | bytes 557056 | tf_op jit(solution)/shard_map/all_gather | solution.py:22
  500.8 198.7 %all-gather.16.cloned.1.call-done = bf16[32768,256]{0,1:T(8,128)(2,1)} async-done(((bf16[2048,256]{0,1:T(8,128)(2,1)}), bf16[32768,256]{0,1:T(8,128)(2,1)}) %all-gather.16.cloned.1.call-update) | async-done | bytes 16777232 | tf_op jit(solution)/shard_map/all_gather | solution.py:12
  699.5 15.1 %copy.45 = bf16[32,8,16,2048]{3,2,1,0:T(8,128)(2,1)S(1)} copy(bf16[32,8,16,2048]{3,1,2,0:T(8,128)(2,1)} %bitcast.222) | data formatting | bytes 33554432
  714.6 8.1 bitcast_reduce_fusion.1
  725.4 2.3 collective-permute-done.3
  727.7 24.1 %all_gather.44 = bf16[512,512]{1,0:T(8,128)(2,1)S(1)} all-gather(bf16[32,512]{1,0:T(8,128)(2,1)S(1)} %concatenate.25), channel_id=1, replica_groups=mesh['leaf'=32,'front'=16] {'front'}, dimensions={0}, use_global_device_ids=true | all-gather | bytes 557056 | tf_op jit(solution)/shard_map/all_gather | solution.py:22
  760.6 195.8 %all-gather.18.cloned.1.call-done = bf16[32768,256]{0,1:T(8,128)(2,1)} async-done(((bf16[2048,256]{0,1:T(8,128)(2,1)}), bf16[32768,256]{0,1:T(8,128)(2,1)}) %all-gather.18.cloned.1.call-update) | async-done | bytes 16777232 | tf_op jit(solution)/shard_map/all_gather | solution.py:12
  956.4 15.1 %copy.46 = bf16[32,8,16,2048]{3,2,1,0:T(8,128)(2,1)S(1)} copy(bf16[32,8,16,2048]{3,1,2,0:T(8,128)(2,1)} %bitcast.220) | data formatting | bytes 33554432
  971.5 8.1 bitcast_reduce_fusion
  981.5 82.3 %all-gather.10.cloned.1.call-done = bf16[2,2048,768]{2,1,0:T(8,128)(2,1)} async-done(((bf16[2,128,768]{2,1,0:T(8,128)(2,1)}), bf16[2,2048,768]{2,1,0:T(8,128)(2,1)}) %all-gather.10.cloned.1.call-update) | async-done | bytes 6291472 | tf_op jit(solution)/shard_map/all_gather | solution.py:22
  1065.6 2.8 collective-permute-start.4
  1071.8 9.2 all-to-all-start
  1081.2 44.4 %all-to-all-done = bf16[16,128,256]{2,1,0:T(8,128)(2,1)S(1)} async-done(((bf16[16,128,256]{2,1,0:T(8,128)(2,1)}), bf16[16,128,256]{2,1,0:T(8,128)(2,1)S(1)}, u32[]{:S(2)}, u32[]{:S(2)}) %all-to-all-start) | async-done | bytes 1048608 | tf_op jit(solution)/shard_map/all_to_all | solution.py:39
  1127.5 3.3 fusion.21
  1130.8 8.6 collective-permute-start.6
  1141.3 3.6 collective-permute-done.5
  1145.2 59.2 %all_to_all.15 = bf16[16,128,256]{2,1,0:T(8,128)(2,1)S(1)} all-to-all(bf16[16,128,256]{2,1,0:T(8,128)(2,1)S(1)} %broadcast_in_dim.87), channel_id=1, replica_groups=mesh['leaf'=32,'front'=16] {'front'}, dimensions={0} | all-to-all | bytes 2097152 | tf_op jit(solution)/shard_map/all_to_all | solution.py:39
  1206.3 3.3 fusion.19
  1211.5 3.7 collective-permute-done.7
  1216.4 6.9 all-to-all-start.2
  1224.4 49.5 %all-to-all-done.2 = bf16[16,128,256]{2,1,0:T(8,128)(2,1)S(1)} async-done(((bf16[16,128,256]{2,1,0:T(8,128)(2,1)}), bf16[16,128,256]{2,1,0:T(8,128)(2,1)S(1)}, u32[]{:S(2)}, u32[]{:S(2)}) %all-to-all-start.2) | async-done | bytes 1048608 | tf_op jit(solution)/shard_map/all_to_all | solution.py:39
  1275.9 3.3 fusion.22
  (132 shorter events, 46.3 us)
Async XLA Ops:
  7.2 1.6 copy-start.3
  7.2 197.8 %all-gather.12.cloned.1.call-start = ((), (), s32[]{:S(2)}) async-start(), calls=%async_computation.4 | async-start | bytes 17825792 | tf_op jit(solution)/shard_map/all_gather | solution.py:12
  10.3 432.4 %all-gather.14.cloned.1.call-start = ((), (), s32[]{:S(2)}) async-start(), calls=%async_computation.5 | async-start | bytes 17825792 | tf_op jit(solution)/shard_map/all_gather | solution.py:12
  16.7 706.1 %copy-start.11 = (pred[32]{0:T(512)(128)(4,1)}, pred[32]{0:T(512)(128)(4,1)S(1)}, u32[]{:S(2)}) copy-start(pred[32]{0:T(512)(128)(4,1)S(1)} %get-tuple-element.19) | copy-start | bytes 100
  16.7 706.1 %copy-start.13 = (pred[32]{0:T(512)(128)(4,1)}, pred[32]{0:T(512)(128)(4,1)S(1)}, u32[]{:S(2)}) copy-start(pred[32]{0:T(512)(128)(4,1)S(1)} %get-tuple-element.20) | copy-start | bytes 100
  16.7 737.4 %copy-start.15 = (pred[128]{0:T(512)(128)(4,1)}, pred[128]{0:T(512)(128)(4,1)S(1)}, u32[]{:S(2)}) copy-start(pred[128]{0:T(512)(128)(4,1)S(1)} %get-tuple-element.21) | copy-start | bytes 388
  16.7 737.4 %copy-start.17 = (pred[128]{0:T(512)(128)(4,1)}, pred[128]{0:T(512)(128)(4,1)S(1)}, u32[]{:S(2)}) copy-start(pred[128]{0:T(512)(128)(4,1)S(1)} %get-tuple-element.22) | copy-start | bytes 388
  205.0 12.7 copy-start.9
  214.2 30.0 %copy-start = (bf16[1,2,128,2048]{3,2,1,0:T(8,128)(2,1)S(1)}, bf16[1,2,128,2048]{3,2,1,0:T(8,128)(2,1)}, u32[]{:S(2)}) copy-start(bf16[1,2,128,2048]{3,2,1,0:T(8,128)(2,1)} %param.24) | copy-start | bytes 3145732
  214.2 4.3 collective-permute-start
  242.4 2.1 copy-start.1
  242.5 2.1 copy-start.2
  246.1 453.4 %all-gather.16.cloned.1.call-start = ((), (), s32[]{:S(2)}) async-start(), calls=%async_computation.6 | async-start | bytes 17825792 | tf_op jit(solution)/shard_map/all_gather | solution.py:12
  466.3 5.6 collective-permute-start.2
  468.9 3.8 collective-permute-start.1
  500.6 455.8 %all-gather.18.cloned.1.call-start = ((), (), s32[]{:S(2)}) async-start(), calls=%async_computation.7 | async-start | bytes 17825792 | tf_op jit(solution)/shard_map/all_gather | solution.py:12
  723.2 4.5 collective-permute-start.3
  754.8 3.9 copy-start.5
  757.1 306.7 %all-gather.10.cloned.1.call-start = ((), (), s32[]{:S(2)}) async-start(), calls=%async_computation.3 | async-start | bytes 6684672 | tf_op jit(solution)/shard_map/all_gather | solution.py:22
  971.5 8.2 copy-start.16
  971.5 8.2 copy-start.18
  971.5 8.6 copy-start.10
  1065.6 15.5 %copy-start.20 = (s32[1,2,512]{2,1,0:T(2,128)S(1)}, s32[1,2,512]{2,1,0:T(2,128)}, u32[]{:S(2)}) copy-start(s32[1,2,512]{2,1,0:T(2,128)} %param.27) | copy-start | bytes 12292
  1065.6 5.0 collective-permute-start.4
  1071.8 53.7 %all-to-all-start = ((bf16[16,128,256]{2,1,0:T(8,128)(2,1)}), bf16[16,128,256]{2,1,0:T(8,128)(2,1)S(1)}, u32[]{:S(2)}, u32[]{:S(2)}) async-start(bf16[16,128,256]{2,1,0:T(8,128)(2,1)} %broadcast_in_dim.86), calls=%async_computation | async-start | bytes 2097152 | tf_op jit(solution)/shard_map/all_to_all | solution.py:39
  1130.8 10.5 collective-permute-start.6
  1139.3 5.6 collective-permute-start.5
  1209.6 13.8 %copy-start.7 = (bf16[32,256]{1,0:T(8,128)(2,1)S(1)}, bf16[32,256]{1,0:T(8,128)(2,1)}, u32[]{:S(2)}) copy-start(bf16[32,256]{1,0:T(8,128)(2,1)} %gather_fusion.7) | copy-start | bytes 49156
  1209.6 13.8 %copy-start.12 = (pred[32]{0:T(512)(128)(4,1)S(1)}, pred[32]{0:T(512)(128)(4,1)}, u32[]{:S(2)}) copy-start(pred[32]{0:T(512)(128)(4,1)} %copy-done.11) | copy-start | bytes 100
  1209.6 13.8 %copy-start.14 = (pred[32]{0:T(512)(128)(4,1)S(1)}, pred[32]{0:T(512)(128)(4,1)}, u32[]{:S(2)}) copy-start(pred[32]{0:T(512)(128)(4,1)} %copy-done.13) | copy-start | bytes 100
  1209.6 5.6 collective-permute-start.7
  1216.4 57.5 %all-to-all-start.2 = ((bf16[16,128,256]{2,1,0:T(8,128)(2,1)}), bf16[16,128,256]{2,1,0:T(8,128)(2,1)S(1)}, u32[]{:S(2)}, u32[]{:S(2)}) async-start(bf16[16,128,256]{2,1,0:T(8,128)(2,1)} %broadcast_in_dim.88), calls=%async_computation.2 | async-start | bytes 2097152 | tf_op jit(solution)/shard_map/all_to_all | solution.py:39
  (4 other events, 4.8 us)
Sparse Core Ops, SparseCore 0:
  10.4 194.5 all-gather.11
  246.2 196.4 all-gather.13
  500.7 198.7 all-gather.15
  757.2 199.2 all-gather.17
  981.6 82.0 all-gather.9
